TPU v7x, 32 devices: a whole 2x2x4 slice. The times are simulated.
32 devices in a mesh: groups: 2 (over y), dp: 4 (over z), mp: 4 (over x, core).
Axes of the slice: x: 2, y: 2, z: 4, core: 2. Of those that a mesh axis runs over, the one named last changes fastest.
Arguments:
- tile_rows: bfloat16 [128, 32, 1280], P(('groups', 'dp'), None, 'mp'), parts along dimension 0, may hold values from -6 to 6
- tile_count: int32 [128], P(('groups', 'dp')), parts along dimension 0, may hold values from 1 to 4, as said below
- tile_order: int32 [128], P(('groups', 'dp')), parts along dimension 0, may hold values from 0 to 3, as said below
- route: int32 [128, 1], P(('groups', 'dp')), parts along dimension 0, may hold values from 0 to 3; in each aligned block of 16 rows (0 to 15, 16 to 31, ...) at most 8 rows name the same one
- tile_embed: bfloat16 [16, 1280], P(None, 'mp'), may hold values from -3 to 3
- norm_gain: float32 [1280], replicated, may hold values from 0.5 to 2
- norm_bias: float32 [1280], replicated, may hold values from -3 to 3
- w_qkv: bfloat16 [1280, 3, 1280], P(None, None, 'mp'), may hold values from -3 to 3
- w_out: bfloat16 [1280, 1280], P('mp'), may hold values from -0.15625 to 0.15625
- w_proj: bfloat16 [1280, 8192], P(None, 'mp'), may hold values from -0.15625 to 0.15625
- w_kv: bfloat16 [8192, 2048], P('mp', 'dp'), may hold values from -0.0625 to 0.0625
- key_gain: float32 [128], replicated, may hold values from 0.5 to 2
Outputs:
- cross_kv: bfloat16 [256, 32, 2048], P(('groups', 'dp', 'mp')), parts along dimension 0
There are 2 independent parts, one for each index of `groups`. A program takes and returns all parts, laid end to end along the dimension named above; an argument that names none is the same for every part. Nothing has to cross between parts.
Inputs may be any that keep to these rules, and one draw needn't show every extreme that they name: `tile_count`: tiles of one image stand in consecutive slots of one index of dp; the first image of every index of dp has 4 tiles, and the last may be cut at the end of its slots. `tile_order`: counts 0, 1 and so on along the tiles of one image. `route`: the 16 tiles of one index of dp name each destination at most 8 times; in some index of dp some destination is named exactly 8 times.
All inputs are finite; a program needn't handle non-finite values.
Results may differ from a plain program's by a relative error of at most 0.019.
Values may be sent and summed in bfloat16 or wider, within the bound.
A program may use at most 128 MiB of HBM per device.

v0:
```python
import math

import jax
import jax.numpy as jnp
from jax import lax
from jax.sharding import PartitionSpec as P

HD = 80
KVD = 1024
DEC_HD = 128
MAXT = 4


def per_device(
    tile_rows,
    tile_count,
    tile_order,
    route,
    tile_embed,
    norm_gain,
    norm_bias,
    w_qkv,
    w_out,
    w_proj,
    w_kv,
    key_gain,
):
    tiles, patches, local_width = tile_rows.shape
    peers = lax.axis_size("dp")
    models = lax.axis_size("mp")
    cap = 2 * tiles // peers
    f32, bf16 = jnp.float32, jnp.bfloat16

    part = lax.dot_general(w_kv, w_proj, (((0,), (1,)), ((), ())), preferred_element_type=f32)
    part = lax.psum_scatter(part.astype(bf16), "mp", scatter_dimension=0, tiled=True)
    w_all = lax.all_gather(part, ("dp", "mp"), axis=0, tiled=True)
    out_all = lax.all_gather(w_out, "mp", axis=0, tiled=True)

    lookup = (tile_count - 1) * MAXT + tile_order
    lookup_hot = (lookup[:, None] == jnp.arange(MAXT * MAXT)[None, :]).astype(bf16)
    table_rows = jnp.dot(lookup_hot, tile_embed, preferred_element_type=f32)
    embedded = (tile_rows.astype(f32) + table_rows[:, None, :]).astype(bf16)
    full_rows = lax.all_gather(
        embedded.reshape(tiles * patches, local_width), "mp", axis=1, tiled=True
    )
    full_float = full_rows.astype(f32)
    row_mean = jnp.mean(full_float, axis=-1, keepdims=True)
    centred = full_float - row_mean
    row_var = jnp.mean(centred * centred, axis=-1, keepdims=True)
    normed = (centred * lax.rsqrt(row_var + 1e-05) * norm_gain + norm_bias).astype(bf16)
    width = full_rows.shape[1]
    head_width = w_qkv.shape[2]
    heads = head_width // HD
    qkv = jnp.dot(
        normed, w_qkv.reshape(width, 3 * head_width), preferred_element_type=f32
    ).astype(bf16)
    qkv = qkv.reshape(tiles, patches, 3, heads, HD)
    scores = jnp.einsum(
        "sqhe,skhe->shqk", qkv[:, :, 0], qkv[:, :, 1], preferred_element_type=f32
    ) / math.sqrt(HD)
    weights = jax.nn.softmax(scores, axis=-1).astype(bf16)
    context = jnp.einsum(
        "shqk,skhe->sqhe", weights, qkv[:, :, 2], preferred_element_type=f32
    ).astype(bf16)

    destination = route[:, 0]
    dest_hot = (destination[:, None] == jnp.arange(peers)[None, :]).astype(jnp.int32)
    earlier = jnp.cumsum(dest_hot, axis=0) - dest_hot
    position = jnp.sum(earlier * dest_hot, axis=1)
    target = destination * cap + position
    placing = target[:, None] == jnp.arange(peers * cap)[None, :]
    place_t = placing.astype(bf16).T
    occupied = jnp.sum(placing.astype(jnp.int32), axis=0).reshape(peers, 1, cap)
    occupied = jnp.broadcast_to(occupied, (peers, 1, cap))

    def send(values):
        rows = jnp.dot(
            place_t, values.reshape(tiles, patches * local_width), preferred_element_type=f32
        ).astype(bf16).reshape(peers, cap, patches * local_width)
        rows = lax.all_to_all(rows, "dp", split_axis=0, concat_axis=0, tiled=True)
        rows = lax.all_to_all(rows, "mp", split_axis=0, concat_axis=0, tiled=True)
        rows = rows.reshape(models, cap * patches, local_width)
        return rows.transpose(1, 0, 2).reshape(cap * patches, models * local_width)

    filled = lax.all_to_all(occupied, "dp", split_axis=0, concat_axis=0, tiled=True)
    used = lax.dynamic_index_in_dim(filled, lax.axis_index("mp"), 0, keepdims=False)[0] > 0
    ctx = send(context)
    emb = send(embedded)
    attended = jnp.dot(ctx, out_all, preferred_element_type=f32)
    encoded = (emb.astype(f32) + attended).astype(bf16)
    projected = lax.dot_general(
        encoded, w_all, (((1,), (1,)), ((), ())), preferred_element_type=f32
    )
    rows = cap * patches
    key_part = projected[:, :KVD].reshape(rows, KVD // DEC_HD, DEC_HD)
    key_scale = lax.rsqrt(jnp.mean(key_part * key_part, axis=-1, keepdims=True) + 1e-06)
    key_part = (key_part * key_scale * key_gain).reshape(rows, KVD)
    finished = jnp.concatenate([key_part, projected[:, KVD:]], axis=1)
    finished = finished.reshape(cap, patches, projected.shape[1])
    finished = jnp.where(used[:, None, None], finished, 0.0)
    return finished.astype(bf16)


def solution(mesh):
    return jax.shard_map(
        per_device,
        mesh=mesh,
        in_specs=(
            P(("groups", "dp"), None, "mp"),
            P(("groups", "dp")),
            P(("groups", "dp")),
            P(("groups", "dp"), None),
            P(None, "mp"),
            P(),
            P(),
            P(None, None, "mp"),
            P("mp", None),
            P(None, "mp"),
            P("mp", "dp"),
            P(),
        ),
        out_specs=P(("groups", "dp", "mp"), None, None),
        check_vma=False,
    )
```

profile of v0, /device:TPU:9, one launch (start us, length us, event | category | flops | bytes accessed | tf_op | source)
XLA Modules:
  0.0 191.0 jit_solution(5625162831710159908)
XLA Ops:
  6.5 0.0 copy-start
  6.5 0.0 reduce-scatter.2.cloned.1.call-start
  6.6 7.3 %convolution_convert_fusion.2 = bf16[512,1280]{1,0:T(8,128)(2,1)} fusion(bf16[2048,512]{1,0:T(8,128)(2,1)} %param.22, bf16[1280,2048]{1,0:T(8,128)(2,1)} %param.21), kind=kOutput, calls=%fused_computation.9 | convolution fusion | flops 2685009920 | bytes 8650752 | tf_op jit(solution)/shard_map/dot_general | solution.py:34
  13.9 0.0 reduce-scatter.2.cloned.1.call-update
  13.9 0.0 all-gather.4.cloned.1.call-start
  13.9 0.0 copy-done.8
  14.0 0.2 fusion.23
  14.2 0.0 copy-done.2
  14.2 0.1 add_convert_fusion
  14.3 0.9 copy.72
  15.2 0.0 all-gather.4.cloned.1.call-update
  15.2 0.0 all-gather.6.cloned.1.call-start
  15.2 0.7 all-gather.6.cloned.1.call-update
  15.9 0.0 all-gather.8.cloned.1.call-start
  16.0 25.8 %reduce-scatter.2.cloned.1.call-done = bf16[128,1280]{1,0:T(8,128)(2,1)} async-done(((bf16[512,1280]{1,0:T(8,128)(2,1)}), bf16[128,1280]{1,0:T(8,128)(2,1)}) %reduce-scatter.2.cloned.1.call-update) | async-done | bytes 327696 | tf_op jit(solution)/shard_map/reduce_scatter | solution.py:35
  41.8 0.0 all-gather.8.cloned.1.call-update
  41.8 0.0 copy-done.3
  41.8 0.1 fusion.22
  41.9 0.2 select_reduce_fusion
  42.1 0.1 convert_reduce_fusion.1
  42.2 0.7 reshape.80
  42.9 4.6 %all-to-all-start = ((s32[4,1,8]{2,1,0:T(1,128)}), s32[4,1,8]{2,1,0:T(1,128)S(1)}, u32[]{:S(2)}, u32[]{:S(2)}) async-start(s32[4,1,8]{2,1,0:T(1,128)} %bitcast.3), calls=%async_computation | async-start | bytes 4096 | tf_op jit(solution)/shard_map/all_to_all | solution.py:85
  47.4 0.4 reshape.81
  47.8 1.3 fusion.1
  49.1 12.9 %all-gather.4.cloned.1.call-done = bf16[512,1280]{0,1:T(8,128)(2,1)} async-done(((bf16[512,320]{0,1:T(8,128)(2,1)}), bf16[512,1280]{0,1:T(8,128)(2,1)}) %all-gather.4.cloned.1.call-update) | async-done | bytes 1310736 | tf_op jit(solution)/shard_map/all_gather | solution.py:43
  62.0 1.7 convert_reduce_fusion
  63.7 0.0 copy-done.1
  63.7 0.4 fusion.5
  64.2 0.0 all-to-all-done
  64.2 4.6 %all-to-all-start.1 = ((bf16[4,8,10240]{2,1,0:T(8,128)(2,1)}), bf16[4,8,10240]{2,1,0:T(8,128)(2,1)}, u32[]{:S(2)}, u32[]{:S(2)}) async-start(bf16[4,8,10240]{2,1,0:T(8,128)(2,1)} %fusion.1), calls=%async_computation.1 | async-start | bytes 1310720 | tf_op jit(solution)/shard_map/all_to_all | solution.py:80
  68.8 0.0 copy-done
  68.8 0.0 copy-done.7
  68.8 3.9 %convolution_convert_fusion.3 = bf16[512,960]{0,1:T(8,128)(2,1)} fusion(bf16[1280,960]{0,1:T(8,128)(2,1)S(1)} %bitcast.61, bf16[512,1280]{0,1:T(8,128)(2,1)} %all-gather.4.cloned.1.call-done, f32[1280]{0:T(1024)S(1)} %copy-done.6, f32[1280]{0:T(1024)S(1)} %copy-done.7, f32[512]{0:T(512)S(1)} %add_rsqrt_fusion.1, f32[512]{0:T(512)S(1)} %broadcast_multiply_fusion), kind=kOutput, calls=%fused_computation.19 | convolution fusion | flops 1262714880 | bytes 4765696 | tf_op jit(solution)/shard_map/dot_general | solution.py:54
  72.7 1.5 copy.73
  74.2 2.5 %reshape.85 = bf16[16,32,3,4,80]{4,3,2,1,0:T(4,128)(2,1)} reshape(bf16[512,960]{1,0:T(8,128)(2,1)S(1)} %copy.73) | data formatting | bytes 1966080 | tf_op jit(solution)/shard_map/reshape | solution.py:57
  76.6 3.0 %fusion.30 = (bf16[16,32,1,4,80]{4,3,2,1,0:T(4,128)(2,1)S(1)}, bf16[16,32,1,4,80]{4,3,2,1,0:T(4,128)(2,1)}, bf16[16,32,1,4,80]{4,3,2,1,0:T(4,128)(2,1)S(1)}) fusion(bf16[16,32,3,4,80]{4,3,2,1,0:T(4,128)(2,1)} %reshape.85), kind=kLoop, calls=%fused_computation.58 | loop fusion | bytes 1966080 | tf_op jit(solution)/shard_map/slice | solution.py:59
  79.6 1.4 convolution_multiply_fusion
  81.0 1.6 all-to-all-done.1
  82.6 5.5 %all-to-all-start.2 = ((bf16[4,8,10240]{2,1,0:T(8,128)(2,1)}), bf16[4,8,10240]{2,1,0:T(8,128)(2,1)}, u32[]{:S(2)}, u32[]{:S(2)}) async-start(bf16[4,8,10240]{2,1,0:T(8,128)(2,1)} %all-to-all-done.1), calls=%async_computation.2 | async-start | bytes 1310720 | tf_op jit(solution)/shard_map/all_to_all | solution.py:81
  88.1 0.6 fusion.31
  88.7 2.2 %fusion.18 = bf16[16,32,4,80]{3,1,2,0:T(8,128)(2,1)S(1)} fusion(bf16[16,32,1,4,80]{4,3,2,1,0:T(4,128)(2,1)} %get-tuple-element.8, f32[16,4,32]{2,1,0:T(4,128)S(1)} %fusion.31, f32[16,4,32,32]{2,3,1,0:T(8,128)} %convolution_multiply_fusion), kind=kOutput, calls=%fused_computation.27 | convolution fusion | flops 10848287 | bytes 925696 | tf_op jit(solution)/shard_map/shqk,skhe->sqhe/dot_general | solution.py:62
  91.0 0.3 copy.78
  91.2 0.0 copy-start.4
  91.3 0.8 reshape.86
  92.1 0.4 fusion.2
  92.5 5.6 %all-to-all-done.2 = bf16[4,8,10240]{2,1,0:T(8,128)(2,1)} async-done(((bf16[4,8,10240]{2,1,0:T(8,128)(2,1)}), bf16[4,8,10240]{2,1,0:T(8,128)(2,1)}, u32[]{:S(2)}, u32[]{:S(2)}) %all-to-all-start.2) | async-done | bytes 655392 | tf_op jit(solution)/shard_map/all_to_all | solution.py:81
  98.2 31.9 %all_to_all.25 = bf16[4,8,10240]{2,1,0:T(8,128)(2,1)} all-to-all(bf16[4,8,10240]{2,1,0:T(8,128)(2,1)S(1)} %fusion.2), channel_id=1, replica_groups=mesh['groups'=2,'dp'=4,'mp'=4] {'dp'}, dimensions={0} | all-to-all | bytes 1310720 | tf_op jit(solution)/shard_map/all_to_all | solution.py:80
  130.1 5.0 %all-to-all-start.4 = ((bf16[4,8,10240]{2,1,0:T(8,128)(2,1)}), bf16[4,8,10240]{2,1,0:T(8,128)(2,1)}, u32[]{:S(2)}, u32[]{:S(2)}) async-start(bf16[4,8,10240]{2,1,0:T(8,128)(2,1)} %all_to_all.25), calls=%async_computation.4 | async-start | bytes 1310720 | tf_op jit(solution)/shard_map/all_to_all | solution.py:81
  135.1 2.9 %reshape.91 = f32[4,256,320]{2,1,0:T(8,128)} reshape(bf16[4,8,10240]{2,1,0:T(8,128)(2,1)} %all-to-all-done.2) | data formatting | bytes 1966080 | tf_op jit(solution)/shard_map/convert_element_type | solution.py:90
  137.9 3.0 %copy.71 = f32[256,4,320]{0,2,1:T(8,128)} copy(f32[256,4,320]{2,0,1:T(8,128)} %bitcast.62) | data formatting | bytes 2621440 | tf_op jit(solution)/shard_map/convert_element_type | solution.py:90
  140.9 2.8 %copy.80 = f32[256,1280]{1,0:T(8,128)} copy(f32[256,1280]{0,1:T(8,128)} %bitcast.63) | data formatting | bytes 2621440 | tf_op jit(solution)/shard_map/convert_element_type | solution.py:90
  143.7 7.9 %all-to-all-done.4 = bf16[4,8,10240]{2,1,0:T(8,128)(2,1)} async-done(((bf16[4,8,10240]{2,1,0:T(8,128)(2,1)}), bf16[4,8,10240]{2,1,0:T(8,128)(2,1)}, u32[]{:S(2)}, u32[]{:S(2)}) %all-to-all-start.4) | async-done | bytes 655392 | tf_op jit(solution)/shard_map/all_to_all | solution.py:81
  151.6 2.0 %reshape.88 = bf16[4,256,320]{2,1,0:T(8,128)(2,1)S(1)} reshape(bf16[4,8,10240]{2,1,0:T(8,128)(2,1)} %all-to-all-done.4) | data formatting | bytes 1310720 | tf_op jit(solution)/shard_map/reshape | solution.py:82
  153.6 1.1 copy.79
  154.8 14.8 %all-gather.8.cloned.1.call-done = bf16[2048,1280]{1,0:T(8,128)(2,1)} async-done(((bf16[128,1280]{1,0:T(8,128)(2,1)}), bf16[2048,1280]{1,0:T(8,128)(2,1)}) %all-gather.8.cloned.1.call-update) | async-done | bytes 5242896 | tf_op jit(solution)/shard_map/all_gather | solution.py:36
  169.6 7.8 %fusion.20 = f32[256,2048]{1,0:T(8,128)} fusion(bf16[2048,1280]{1,0:T(8,128)(2,1)} %all-gather.8.cloned.1.call-done, f32[256,1280]{1,0:T(8,128)} %copy.80, bf16[256,1280]{0,1:T(8,128)(2,1)} %bitcast.70, bf16[1280,1280]{1,0:T(8,128)(2,1)} %all-gather.6.cloned.1.call-done), kind=kOutput, calls=%fused_computation.33 | convolution fusion | flops 2181693440 | bytes 12582912 | tf_op jit(solution)/shard_map/dot_general | solution.py:91
  177.3 1.3 multiply_bitcast_fusion
  178.7 0.2 copy.87
  178.9 1.0 reduce_sum.62
  179.9 1.0 copy.81
  180.8 0.1 copy.82
  181.0 0.3 mul.69
  181.3 1.9 fusion.19
  183.2 1.3 fusion.10
  (21 shorter events, 0.1 us)
Async XLA Ops:
  6.5 62.2 %copy-start = (bf16[1280,3,320]{0,2,1:T(8,128)(2,1)S(1)}, bf16[1280,3,320]{0,2,1:T(8,128)(2,1)}, u32[]{:S(2)}) copy-start(bf16[1280,3,320]{0,2,1:T(8,128)(2,1)} %param.19) | copy-start | bytes 7372804
  6.5 7.4 %copy-start.8 = (s32[16]{0:T(128)S(1)}, s32[16]{0:T(128)}, u32[]{:S(2)}) copy-start(s32[16]{0:T(128)} %param.14) | copy-start | bytes 196
  6.5 7.4 %copy-start.9 = (s32[16]{0:T(128)S(1)}, s32[16]{0:T(128)}, u32[]{:S(2)}) copy-start(s32[16]{0:T(128)} %param.13) | copy-start | bytes 196
  6.5 7.4 %copy-start.5 = (bf16[16,320]{1,0:T(8,128)(2,1)S(1)}, bf16[16,320]{1,0:T(8,128)(2,1)}, u32[]{:S(2)}) copy-start(bf16[16,320]{1,0:T(8,128)(2,1)} %param.16) | copy-start | bytes 30724
  6.5 7.6 %copy-start.2 = (bf16[16,32,320]{2,1,0:T(8,128)(2,1)S(1)}, bf16[16,32,320]{2,1,0:T(8,128)(2,1)}, u32[]{:S(2)}) copy-start(bf16[16,32,320]{2,1,0:T(8,128)(2,1)} %param.12) | copy-start | bytes 983044
  6.5 35.2 %reduce-scatter.2.cloned.1.call-start = ((), (), s32[]{:S(2)}) async-start(), calls=%async_computation.8 | async-start | bytes 1638400 | tf_op jit(solution)/shard_map/reduce_scatter | solution.py:35
  13.9 27.9 %copy-start.3 = (s32[16,1]{0,1:T(1,128)S(1)}, s32[16,1]{0,1:T(1,128)}, u32[]{:S(2)}) copy-start(s32[16,1]{0,1:T(1,128)} %param.15) | copy-start | bytes 196
  13.9 48.2 %all-gather.4.cloned.1.call-start = ((), (), s32[]{:S(2)}) async-start(), calls=%async_computation.6 | async-start | bytes 1638400 | tf_op jit(solution)/shard_map/all_gather | solution.py:43
  15.2 139.6 %all-gather.6.cloned.1.call-start = ((), (), s32[]{:S(2)}) async-start(), calls=%async_computation.7 | async-start | bytes 4096000 | tf_op jit(solution)/shard_map/all_gather | solution.py:37
  15.9 153.6 %all-gather.8.cloned.1.call-start = ((), (), s32[]{:S(2)}) async-start(), calls=%async_computation.9 | async-start | bytes 5570560 | tf_op jit(solution)/shard_map/all_gather | solution.py:36
  42.9 21.3 %all-to-all-start = ((s32[4,1,8]{2,1,0:T(1,128)}), s32[4,1,8]{2,1,0:T(1,128)S(1)}, u32[]{:S(2)}, u32[]{:S(2)}) async-start(s32[4,1,8]{2,1,0:T(1,128)} %bitcast.3), calls=%async_computation | async-start | bytes 4096 | tf_op jit(solution)/shard_map/all_to_all | solution.py:85
  62.0 1.7 copy-start.1
  62.0 6.7 %copy-start.6 = (f32[1280]{0:T(1024)S(1)}, f32[1280]{0:T(1024)}, u32[]{:S(2)}) copy-start(f32[1280]{0:T(1024)} %param.18) | copy-start | bytes 15364
  62.0 6.7 %copy-start.7 = (f32[1280]{0:T(1024)S(1)}, f32[1280]{0:T(1024)}, u32[]{:S(2)}) copy-start(f32[1280]{0:T(1024)} %param.17) | copy-start | bytes 15364
  64.2 18.4 %all-to-all-start.1 = ((bf16[4,8,10240]{2,1,0:T(8,128)(2,1)}), bf16[4,8,10240]{2,1,0:T(8,128)(2,1)}, u32[]{:S(2)}, u32[]{:S(2)}) async-start(bf16[4,8,10240]{2,1,0:T(8,128)(2,1)} %fusion.1), calls=%async_computation.1 | async-start | bytes 1310720 | tf_op jit(solution)/shard_map/all_to_all | solution.py:80
  82.6 15.6 %all-to-all-start.2 = ((bf16[4,8,10240]{2,1,0:T(8,128)(2,1)}), bf16[4,8,10240]{2,1,0:T(8,128)(2,1)}, u32[]{:S(2)}, u32[]{:S(2)}) async-start(bf16[4,8,10240]{2,1,0:T(8,128)(2,1)} %all-to-all-done.1), calls=%async_computation.2 | async-start | bytes 1310720 | tf_op jit(solution)/shard_map/all_to_all | solution.py:81
  91.2 43.8 %copy-start.4 = (f32[128]{0:T(128)S(1)}, f32[128]{0:T(128)}, u32[]{:S(2)}) copy-start(f32[128]{0:T(128)} %param.23) | copy-start | bytes 1540
  130.1 21.6 %all-to-all-start.4 = ((bf16[4,8,10240]{2,1,0:T(8,128)(2,1)}), bf16[4,8,10240]{2,1,0:T(8,128)(2,1)}, u32[]{:S(2)}, u32[]{:S(2)}) async-start(bf16[4,8,10240]{2,1,0:T(8,128)(2,1)} %all_to_all.25), calls=%async_computation.4 | async-start | bytes 1310720 | tf_op jit(solution)/shard_map/all_to_all | solution.py:81
Sparse Core Ops, SparseCore 0:
  14.0 27.7 reduce-scatter.1
  43.4 18.5 all-gather.3
  63.7 29.5 all-gather.5
  95.7 73.7 all-gather.7
where the time goes:
time: 193 us; the launch traced here: 191 us
  waiting for transfers between devices  69.4 us (36%)
  blocking collectives  31.9 us (17%)
  matrix products  25 us (13%)
  local copies, waits for them, and re-layouts  23.5 us (12%)
  starting transfers between devices  19.8 us (10%)
  between operations  13.3 us (7%)
  other arithmetic  8.07 us (4%)
    all_to_all x1, blocking collectives, send(): rows = lax.all_to_all(rows, 'dp', split_axis=0, concat_axis=0, tiled=True)  31.9 us
    reduce_scatter x1, waiting for transfers between devices, per_device(): lax.psum_scatter(part.astype(bf16), 'mp', scatter_dimension=0, tiled=True)  25.8 us
    all_gather x1, waiting for transfers between devices, per_device(): w_all = lax.all_gather(part, ('dp', 'mp'), axis=0, tiled=True)  14.8 us
    all_to_all x2, waiting for transfers between devices, send(): rows = lax.all_to_all(rows, 'mp', split_axis=0, concat_axis=0, tiled=True)  13.5 us
    all_gather x1, waiting for transfers between devices, per_device(): lax.all_gather(embedded.reshape(tiles * patches, local_width), 'mp', axis...  12.9 us
    all_to_all x2, starting transfers between devices, send(): rows = lax.all_to_all(rows, 'mp', split_axis=0, concat_axis=0, tiled=True)  10.5 us
    convert_element_type x3, local copies, waits for them, and re-layouts, per_device(): encoded = (emb.astype(f32) + attended).astype(bf16)  8.67 us
    dot_general x1, matrix products, per_device(): lax.dot_general(encoded, w_all, (((1,), (1,)), ((), ())), preferred_eleme...  7.78 us
  transfers between devices with their start and end apart: 8, of which 6 were waited for; matrix products, arithmetic and copies ran while one was open for 18% of the time, Pallas kernels for 0%

commit v1 on v0

--- a/solution.py
+++ b/solution.py
@@ -2,7 +2,10 @@
 
 import jax
 import jax.numpy as jnp
+import numpy as np
 from jax import lax
+from jax.experimental import pallas as pl
+from jax.experimental.pallas import tpu as pltpu
 from jax.sharding import PartitionSpec as P
 
 HD = 80
@@ -101,9 +104,300 @@
     return finished.astype(bf16)
 
 
+N = 4
+MESH = pl.DeviceIdType.MESH
+
+
+def selector():
+    table = np.zeros((N * HD, N * 128), np.float32)
+    for head in range(N):
+        for e in range(HD):
+            table[head * HD + e, head * 128 + e] = 1.0
+    return table
+
+
+def kernel(
+    emb_ref, tgt_ref, gain_ref, bias_ref, wqkv_ref, wout_ref, wproj_ref, wkv_ref, kgain_ref,
+    sel_ref, selt_ref, out_ref,
+    embf, ctxs, csend, esend, ctxr, embr, woutf, rssrc, rsbuf, own, wall,
+    es, er, os, orr, rs_s, rs_r, zs, zr, ys, yr, xs, xr, c_s, c_r, cs, cr, ms, mr,
+):
+    f32, bf16 = jnp.float32, jnp.bfloat16
+    g, j, m = lax.axis_index("groups"), lax.axis_index("dp"), lax.axis_index("mp")
+    xp = lax.rem(m + 2, N)
+    cp = m + 1 - 2 * lax.rem(m, 2)
+    xcp = lax.rem(cp + 2, N)
+    rows, lanes = emb_ref.shape
+    blk = wqkv_ref.shape[2]
+    slots = ctxr.shape[1]
+    half = wall.shape[3]
+
+    def copy(src, dst, ssem, rsem, dev):
+        return pltpu.make_async_remote_copy(
+            src_ref=src, dst_ref=dst, send_sem=ssem, recv_sem=rsem,
+            device_id=dev, device_id_type=MESH,
+        )
+
+    barrier = pltpu.get_barrier_semaphore()
+    for k in range(1, N * N):
+        other = lax.rem(j * N + m + k, N * N)
+        pl.semaphore_signal(
+            barrier, inc=1, device_id=(g, other // N, lax.rem(other, N)), device_id_type=MESH
+        )
+    pl.semaphore_signal(barrier, inc=1, device_id=(1 - g, j, m), device_id_type=MESH)
+    pl.semaphore_wait(barrier, N * N)
+
+    pending = []
+
+    def start(c):
+        c.start()
+        pending.append(c)
+
+    start(copy(emb_ref, embf.at[m], es.at[0], er.at[m], (g, j, xp)))
+    start(copy(emb_ref, embf.at[m], es.at[1], er.at[m], (g, j, cp)))
+
+    cols = pl.ds(pl.multiple_of(g * half, half), half)
+    for k in (2, 3, 1, 0):
+        to = lax.rem(m + k, N)
+        prod = jnp.dot(
+            wproj_ref[pl.ds(pl.multiple_of(to * blk, 16), blk), :], wkv_ref[:, cols],
+            preferred_element_type=f32,
+        )
+        if k == 0:
+            own[...] = prod
+        else:
+            rssrc[k] = prod.astype(bf16)
+            start(copy(rssrc.at[k], rsbuf.at[m], rs_s.at[k], rs_r.at[m], (g, j, to)))
+
+    emb_own = emb_ref[...]
+    embf[m] = emb_own
+    tgt = tgt_ref[...]
+    place = lax.broadcasted_iota(jnp.int32, (slots, rows), 0)
+
+    def routed(values, send, recv, ssem, rsem):
+        for d in range(N):
+            hot = (place + d * slots == tgt).astype(f32).astype(bf16)
+            send[d] = jnp.dot(hot, values, preferred_element_type=f32).astype(bf16)
+            here = jnp.logical_and(j == d, m == d)
+
+            @pl.when(here)
+            def _():
+                recv[m] = send[d]
+
+            @pl.when(jnp.logical_not(here))
+            def _():
+                copy(send.at[d], recv.at[m], ssem.at[d], rsem.at[m], (g, d, j)).start()
+
+    def routed_arrived(send, recv, ssem, rsem):
+        for k in range(N):
+            @pl.when(jnp.logical_not(jnp.logical_and(j == m, m == k)))
+            def _():
+                copy(send.at[k], recv.at[k], ssem.at[k], rsem.at[k], (g, j, xp)).wait_recv()
+
+    def routed_sent(send, recv, ssem, rsem):
+        for d in range(N):
+            @pl.when(jnp.logical_not(jnp.logical_and(j == d, m == d)))
+            def _():
+                copy(send.at[d], recv.at[m], ssem.at[d], rsem.at[m], (g, d, j)).wait_send()
+
+    copy(emb_ref, embf.at[xp], es.at[0], er.at[xp], (g, j, xp)).wait_recv()
+    start(copy(embf.at[xp], embf.at[xp], es.at[2], er.at[xp], (g, j, cp)))
+
+    total = own[...]
+    for k in (1, 3, 2):
+        frm = lax.rem(m + k, N)
+        copy(rssrc.at[k], rsbuf.at[frm], rs_s.at[k], rs_r.at[frm], (g, j, frm)).wait_recv()
+        total = total + rsbuf[frm].astype(f32)
+    mine = pl.ds(pl.multiple_of(m * blk, 16), blk)
+    xrow = pl.ds(pl.multiple_of(xp * blk, 16), blk)
+    crow = pl.ds(pl.multiple_of(cp * blk, 16), blk)
+    xcrow = pl.ds(pl.multiple_of(xcp * blk, 16), blk)
+    wall[g, j, mine, :] = total.astype(bf16)
+    unit = wall.at[g, j, mine, :]
+    for k in (1, 3, 2):
+        start(copy(unit, unit, zs.at[k], zr.at[j], (g, lax.rem(j + k, N), m)))
+
+    def spread(gg, jj, at):
+        u = wall.at[gg, jj, mine, :]
+        start(copy(u, u, xs.at[at], xr.at[gg, jj], (g, j, xp)))
+        start(copy(u, u, c_s.at[at], c_r.at[gg, jj], (g, j, cp)))
+
+    start(copy(unit, unit, ys.at[0], yr.at[j], (1 - g, j, m)))
+
+    for b in (cp, xcp):
+        copy(emb_ref, embf.at[b], es.at[0], er.at[b], (g, j, xp)).wait_recv()
+
+    tile = rows // 16
+    step = 4 * tile
+    rid = lax.broadcasted_iota(jnp.int32, (step, step), 0) // tile
+    cid = lax.broadcasted_iota(jnp.int32, (step, step), 1) // tile
+    same = rid == cid
+
+    def encode(r, carry):
+        at = pl.ds(pl.multiple_of(r * step, step), step)
+        x = [embf[n, at, :][:, :blk].astype(f32) for n in range(N)]
+        mean = sum(jnp.sum(v, axis=-1, keepdims=True) for v in x) / (N * blk)
+        x = [v - mean for v in x]
+        var = sum(jnp.sum(v * v, axis=-1, keepdims=True) for v in x) / (N * blk)
+        inv = lax.rsqrt(var + 1e-05)
+        x = [(x[n] * inv * gain_ref[n] + bias_ref[n]).astype(bf16) for n in range(N)]
+        parts = []
+        for k in range(3):
+            acc = jnp.zeros((step, blk), f32)
+            for n in range(N):
+                acc = acc + jnp.dot(
+                    x[n], wqkv_ref[k, n * blk:(n + 1) * blk, :], preferred_element_type=f32
+                )
+            parts.append(
+                jnp.dot(acc.astype(bf16), sel_ref[...], preferred_element_type=f32).astype(bf16)
+            )
+        ctx = jnp.zeros((step, blk), f32)
+        for h in range(N):
+            hs = slice(h * 128, (h + 1) * 128)
+            scores = lax.dot_general(
+                parts[0][:, hs], parts[1][:, hs], (((1,), (1,)), ((), ())),
+                preferred_element_type=f32,
+            ) / math.sqrt(HD)
+            scores = jnp.where(same, scores, -1e30)
+            top = jnp.max(scores, axis=-1, keepdims=True)
+            e = jnp.where(same, jnp.exp(scores - top), 0.0)
+            wts = (e / jnp.sum(e, axis=-1, keepdims=True)).astype(bf16)
+            c = jnp.dot(wts, parts[2][:, hs], preferred_element_type=f32).astype(bf16)
+            ctx = ctx + jnp.dot(c, selt_ref[h * 128:(h + 1) * 128, :], preferred_element_type=f32)
+        ctxs[at, :] = ctx.astype(bf16)
+        return carry
+
+    lax.fori_loop(0, rows // step, encode, 0)
+    routed(ctxs[...], csend, ctxr, cs, cr)
+    routed(emb_own, esend, embr, ms, mr)
+
+    start(copy(wout_ref, woutf.at[m], os.at[0], orr.at[m], (g, j, xp)))
+    start(copy(wout_ref, woutf.at[m], os.at[1], orr.at[m], (g, j, cp)))
+    woutf[m] = wout_ref[...]
+    order = [0, 1, 3, 2]
+    spread(g, j, 0)
+    for k in order[1:]:
+        jj = lax.rem(j + k, N)
+        u = wall.at[g, jj, mine, :]
+        copy(u, u, zs.at[k], zr.at[jj], (g, j, xp)).wait_recv()
+        start(copy(u, u, ys.at[k], yr.at[jj], (1 - g, j, m)))
+        spread(g, jj, k)
+    for k in order:
+        jj = lax.rem(j + k, N)
+        u = wall.at[1 - g, jj, mine, :]
+        copy(u, u, ys.at[k], yr.at[jj], (1 - g, j, m)).wait_recv()
+        spread(1 - g, jj, N + k)
+    copy(wout_ref, woutf.at[xp], os.at[0], orr.at[xp], (g, j, xp)).wait_recv()
+    start(copy(woutf.at[xp], woutf.at[xp], os.at[2], orr.at[xp], (g, j, cp)))
+    units = [(gg, k) for gg in range(2) for k in order]
+    for gg, k in units:
+        ga = g if gg == 0 else 1 - g
+        jj = lax.rem(j + k, N)
+        u = wall.at[ga, jj, xrow, :]
+        copy(u, u, xs.at[gg * N + k], xr.at[ga, jj], (g, j, xp)).wait_recv()
+        start(copy(u, u, c_s.at[8 + gg * N + k], c_r.at[2 + ga, jj], (g, j, cp)))
+
+    routed_arrived(csend, ctxr, cs, cr)
+    routed_arrived(esend, embr, ms, mr)
+    for b in (cp, xcp):
+        copy(wout_ref, woutf.at[b], os.at[0], orr.at[b], (g, j, xp)).wait_recv()
+    enc = []
+    for n in range(N):
+        acc = jnp.zeros((slots, blk), f32)
+        for k in range(N):
+            acc = acc + jnp.dot(ctxr[k], woutf[k, n], preferred_element_type=f32)
+        enc.append((embr[n][:, :blk].astype(f32) + acc).astype(bf16))
+    used = embr[0][:, blk:blk + 1].astype(f32) > 0.5
+
+    for gg, k in units:
+        ga = g if gg == 0 else 1 - g
+        jj = lax.rem(j + k, N)
+        for b, row in ((0, crow), (2, xcrow)):
+            u = wall.at[ga, jj, row, :]
+            copy(u, u, c_s.at[0], c_r.at[b + ga, jj], (g, j, cp)).wait_recv()
+        acc = jnp.zeros((slots, half), f32)
+        for n in range(N):
+            acc = acc + jnp.dot(
+                enc[n], wall[ga, jj, n * blk:(n + 1) * blk, :], preferred_element_type=f32
+            )
+        key = (2 * jj + ga) * half < KVD
+        for s in range(half // DEC_HD):
+            p = acc[:, s * DEC_HD:(s + 1) * DEC_HD]
+            scale = lax.rsqrt(jnp.mean(p * p, axis=-1, keepdims=True) + 1e-06)
+            p = jnp.where(key, p * scale * kgain_ref[...], p)
+            p = jnp.where(used, p, 0.0).astype(bf16)
+            at = pl.ds(pl.multiple_of((2 * jj + ga) * half + s * DEC_HD, DEC_HD), DEC_HD)
+            out_ref[:, at] = p
+
+    for c in pending:
+        c.wait_send()
+    routed_sent(csend, ctxr, cs, cr)
+    routed_sent(esend, embr, ms, mr)
+
+
+def per_device_kernel(
+    tile_rows, tile_count, tile_order, route, tile_embed, norm_gain, norm_bias,
+    w_qkv, w_out, w_proj, w_kv, key_gain,
+):
+    f32, bf16 = jnp.float32, jnp.bfloat16
+    tiles, patches, blk = tile_rows.shape
+    cap = 2 * tiles // N
+    rows, slots = tiles * patches, cap * patches
+    width, columns = w_proj.shape[0], w_kv.shape[1] * N
+    half = w_kv.shape[1] // 2
+    lanes = -(-(blk + 1) // 128) * 128
+    lookup = (tile_count - 1) * MAXT + tile_order
+    lookup_hot = (lookup[:, None] == jnp.arange(MAXT * MAXT)[None, :]).astype(bf16)
+    table_rows = jnp.dot(lookup_hot, tile_embed, preferred_element_type=f32)
+    emb = (tile_rows.astype(f32) + table_rows[:, None, :]).astype(bf16).reshape(rows, blk)
+    emb = jnp.pad(emb, ((0, 0), (0, lanes - blk)), constant_values=1)
+    destination = route[:, 0]
+    dest_hot = (destination[:, None] == jnp.arange(N)[None, :]).astype(jnp.int32)
+    earlier = jnp.cumsum(dest_hot, axis=0) - dest_hot
+    target = destination * cap + jnp.sum(earlier * dest_hot, axis=1)
+    tgt = (target[:, None] * patches + jnp.arange(patches)[None, :]).reshape(1, rows)
+    wqkv = w_qkv.transpose(1, 0, 2)
+    wout = w_out.reshape(blk, N, blk).transpose(1, 0, 2)
+    sel = jnp.asarray(selector(), bf16)
+    selt = jnp.asarray(selector().T, bf16)
+    vm = pl.BlockSpec(memory_space=pltpu.VMEM)
+    sem = pltpu.SemaphoreType.DMA
+    out = pl.pallas_call(
+        kernel,
+        out_shape=jax.ShapeDtypeStruct((slots, columns), bf16),
+        in_specs=[vm] * 11,
+        out_specs=vm,
+        scratch_shapes=[
+            pltpu.VMEM((N, rows, lanes), bf16),
+            pltpu.VMEM((rows, blk), bf16),
+            pltpu.VMEM((N, slots, blk), bf16),
+            pltpu.VMEM((N, slots, lanes), bf16),
+            pltpu.VMEM((N, slots, blk), bf16),
+            pltpu.VMEM((N, slots, lanes), bf16),
+            pltpu.VMEM((N, N, blk, blk), bf16),
+            pltpu.VMEM((N, blk, half), bf16),
+            pltpu.VMEM((N, blk, half), bf16),
+            pltpu.VMEM((blk, half), f32),
+            pltpu.VMEM((2, N, width, half), bf16),
+            sem((3,)), sem((N,)), sem((3,)), sem((N,)),
+            sem((N,)), sem((N,)), sem((N,)), sem((N,)), sem((N,)), sem((N,)),
+            sem((2 * N,)), sem((2, N)), sem((4 * N,)), sem((4, N)),
+            sem((N,)), sem((N,)), sem((N,)), sem((N,)),
+        ],
+        compiler_params=pltpu.CompilerParams(
+            collective_id=0, has_side_effects=True, vmem_limit_bytes=56 << 20
+        ),
+    )(
+        emb, tgt, norm_gain.reshape(N, 1, blk), norm_bias.reshape(N, 1, blk), wqkv, wout,
+        w_proj, w_kv, key_gain.reshape(1, -1), sel, selt,
+    )
+    return out.reshape(cap, patches, columns)
+
+
 def solution(mesh):
+    aligned = mesh.shape["dp"] == N and mesh.shape["mp"] == N and mesh.shape["groups"] == 2
     return jax.shard_map(
-        per_device,
+        per_device_kernel if aligned else per_device,
         mesh=mesh,
         in_specs=(
             P(("groups", "dp"), None, "mp"),

time: 193 us -> 140 us (0.73)
  Pallas kernels: 0 us -> 120 us
  waiting for transfers between devices: 69.4 us -> 0 us
  blocking collectives: 31.9 us -> 0 us
  matrix products: 25 us -> 0.19 us
  starting transfers between devices: 19.8 us -> 0 us
  between operations: 13.3 us -> 0.03 us
  local copies, waits for them, and re-layouts: 23.5 us -> 13.4 us
  other arithmetic: 8.07 us -> 4.24 us
    pallas_call x0 -> x1, Pallas kernels: none -> 120 us  [per_device_kernel(): pl.pallas_call(kernel, out_shape=jax.ShapeDtypeStruct((slots, columns), b...]
    all_to_all x1 -> x0, blocking collectives: 31.9 us -> none  [send(): rows = lax.all_to_all(rows, 'dp', split_axis=0, concat_axis=0, tiled=True)]
    all_gather x3 -> x0, waiting for transfers between devices: 27.7 us -> none  [the longest x1 14.8 us: per_device(): w_all = lax.all_gather(part, ('dp', 'mp'), axis=0, tiled=True)]
    reduce_scatter x1 -> x0, waiting for transfers between devices: 25.8 us -> none  [per_device(): lax.psum_scatter(part.astype(bf16), 'mp', scatter_dimension=0, tiled=True)]
    dot_general x8 -> x1, matrix products: 24.5 us -> 0.19 us  [per_device_kernel(): table_rows = jnp.dot(lookup_hot, tile_embed, preferred_element_type=f32)]
    all_to_all x4 -> x0, starting transfers between devices: 19.7 us -> none  [the longest x2 10.5 us: send(): rows = lax.all_to_all(rows, 'mp', split_axis=0, concat_axis=0, tiled=True)]
    all_to_all x4 -> x0, waiting for transfers between devices: 15.2 us -> none  [the longest x2 13.5 us: send(): rows = lax.all_to_all(rows, 'mp', split_axis=0, concat_axis=0, tiled=True)]
    convert_element_type x5 -> x0, local copies, waits for them, and re-layouts: 10.5 us -> none  [the longest x3 8.67 us: per_device(): encoded = (emb.astype(f32) + attended).astype(bf16)]
  transfers between devices with their start and end apart: 8 -> 0, of which waited for: 6 -> 0; matrix products, arithmetic and copies ran while one was open for 18% -> 0% of each run, Pallas kernels for 0% -> 0%
where the time goes in v1:
time: 140 us; the launch traced here: 138 us
  Pallas kernels  120 us (86%)
  local copies, waits for them, and re-layouts  13.4 us (10%)
  other arithmetic  4.24 us (3%)
    pallas_call x1, Pallas kernels, per_device_kernel(): pl.pallas_call(kernel, out_shape=jax.ShapeDtypeStruct((slots, columns), b...  120 us
    unnamed x6, local copies, waits for them, and re-layouts  5.61 us
    reshape x2, local copies, waits for them, and re-layouts, per_device_kernel(): wout = w_out.reshape(blk, N, blk).transpose(1, 0, 2)  3.6 us

profile of v1, /device:TPU:9, one launch (start us, length us, event | category | flops | bytes accessed | tf_op | source)
XLA Modules:
  0.0 137.7 jit_solution(5744382481421040720)
XLA Ops:
  0.0 0.0 copy-start
  0.0 0.0 copy-start.1
  0.0 0.8 multiply_add_fusion
  0.8 1.4 reshape.46.gain_ref
  2.2 1.4 reshape.47.bias_ref
  3.6 0.7 fusion
  4.3 0.8 select_reduce_fusion
  5.2 0.7 fusion.4
  5.8 0.1 iota_add_fusion
  5.9 0.7 add.51.tgt_ref
  6.6 0.0 copy-done
  6.6 0.2 fusion.1
  6.8 1.1 add_convert_fusion
  7.9 0.8 pad.4.emb_ref
  8.7 2.5 %reshape.48 = bf16[320,4,320]{2,1,0:T(4,128)(2,1)S(1)} reshape(bf16[320,1280]{1,0:T(8,128)(2,1)} %param.22) | data formatting | bytes 1638400 | tf_op jit(solution)/shard_map/reshape | solution.py:360
  11.2 1.1 copy.19
  12.3 0.0 copy-done.1
  12.3 3.3 %copy.16 = bf16[1280,3,320]{2,0,1:T(8,128)(2,1)} copy(bf16[1280,3,320]{0,2,1:T(8,128)(2,1)S(1)} %copy-done.1) | data formatting | bytes 4915200 | tf_op args[7]
  15.6 119.9 %shard_map.136 = bf16[256,2048]{1,0:T(8,128)(2,1)} custom-call(bf16[512,384]{1,0:T(8,128)(2,1)} %pad.4.emb_ref, s32[1,512]{1,0:T(1,128)} %add.51.tgt_ref, f32[4,1,320]{2,1,0:T(1,128)} %reshape.46.gain_ref, f32[4,1,320]{2,1,0:T(1,128)} %reshape.47.bias_ref, bf16[3,1280,320]{2,1,0:T(8,128)(2,1)} %bitcast.17, bf16[4,320,320]{2,1,0:T(8,128)(2,1)} %bitcast.19, ...), custom_call_target="tpu_custom_call" | custom-call | tf_op jit(solution)/shard_map/pallas_call | solution.py:365
  135.4 2.3 %copy.21 = bf16[8,32,2048]{2,1,0:T(8,128)(2,1)} copy(bf16[8,32,2048]{2,1,0:T(8,128)(2,1)} %bitcast.18) | data formatting | bytes 2097152
  (1 shorter events, 0.0 us)
Async XLA Ops:
  0.0 6.6 %copy-start = (bf16[16,320]{1,0:T(8,128)(2,1)S(1)}, bf16[16,320]{1,0:T(8,128)(2,1)}, u32[]{:S(2)}) copy-start(bf16[16,320]{1,0:T(8,128)(2,1)} %param.18) | copy-start | bytes 30724
  0.0 12.3 %copy-start.1 = (bf16[1280,3,320]{0,2,1:T(8,128)(2,1)S(1)}, bf16[1280,3,320]{0,2,1:T(8,128)(2,1)}, u32[]{:S(2)}) copy-start(bf16[1280,3,320]{0,2,1:T(8,128)(2,1)} %param.21) | copy-start | bytes 7372804

commit v2 on v1

--- a/solution.py
+++ b/solution.py
@@ -117,10 +117,10 @@
 
 
 def kernel(
-    emb_ref, tgt_ref, gain_ref, bias_ref, wqkv_ref, wout_ref, wproj_ref, wkv_ref, kgain_ref,
+    emb_ref, trow_ref, gain_ref, bias_ref, wqkv_ref, wout_ref, wproj_ref, wkv_ref, kgain_ref,
     sel_ref, selt_ref, out_ref,
-    embf, ctxs, csend, esend, ctxr, embr, woutf, rssrc, rsbuf, own, wall,
-    es, er, os, orr, rs_s, rs_r, zs, zr, ys, yr, xs, xr, c_s, c_r, cs, cr, ms, mr,
+    embf, asrc, abuf, encg, fin, rssrc, rsbuf, own, wall,
+    es, er, as_s, as_r, rs_s, rs_r, zs, zr, ys, yr, xs, xr, c_s, c_r, gs, gr, fs, fr,
 ):
     f32, bf16 = jnp.float32, jnp.bfloat16
     g, j, m = lax.axis_index("groups"), lax.axis_index("dp"), lax.axis_index("mp")
@@ -129,7 +129,7 @@
     xcp = lax.rem(cp + 2, N)
     rows, lanes = emb_ref.shape
     blk = wqkv_ref.shape[2]
-    slots = ctxr.shape[1]
+    slots = out_ref.shape[0]
     half = wall.shape[3]
 
     def copy(src, dst, ssem, rsem, dev):
@@ -169,36 +169,7 @@
             rssrc[k] = prod.astype(bf16)
             start(copy(rssrc.at[k], rsbuf.at[m], rs_s.at[k], rs_r.at[m], (g, j, to)))
 
-    emb_own = emb_ref[...]
-    embf[m] = emb_own
-    tgt = tgt_ref[...]
-    place = lax.broadcasted_iota(jnp.int32, (slots, rows), 0)
-
-    def routed(values, send, recv, ssem, rsem):
-        for d in range(N):
-            hot = (place + d * slots == tgt).astype(f32).astype(bf16)
-            send[d] = jnp.dot(hot, values, preferred_element_type=f32).astype(bf16)
-            here = jnp.logical_and(j == d, m == d)
-
-            @pl.when(here)
-            def _():
-                recv[m] = send[d]
-
-            @pl.when(jnp.logical_not(here))
-            def _():
-                copy(send.at[d], recv.at[m], ssem.at[d], rsem.at[m], (g, d, j)).start()
-
-    def routed_arrived(send, recv, ssem, rsem):
-        for k in range(N):
-            @pl.when(jnp.logical_not(jnp.logical_and(j == m, m == k)))
-            def _():
-                copy(send.at[k], recv.at[k], ssem.at[k], rsem.at[k], (g, j, xp)).wait_recv()
-
-    def routed_sent(send, recv, ssem, rsem):
-        for d in range(N):
-            @pl.when(jnp.logical_not(jnp.logical_and(j == d, m == d)))
-            def _():
-                copy(send.at[d], recv.at[m], ssem.at[d], rsem.at[m], (g, d, j)).wait_send()
+    embf[m] = emb_ref[...]
 
     copy(emb_ref, embf.at[xp], es.at[0], er.at[xp], (g, j, xp)).wait_recv()
     start(copy(embf.at[xp], embf.at[xp], es.at[2], er.at[xp], (g, j, cp)))
@@ -217,12 +188,14 @@
     for k in (1, 3, 2):
         start(copy(unit, unit, zs.at[k], zr.at[j], (g, lax.rem(j + k, N), m)))
 
-    def spread(gg, jj, at):
+    def spread(gg, jj, at, across=True):
         u = wall.at[gg, jj, mine, :]
-        start(copy(u, u, xs.at[at], xr.at[gg, jj], (g, j, xp)))
+        if across:
+            start(copy(u, u, xs.at[at], xr.at[gg, jj], (g, j, xp)))
         start(copy(u, u, c_s.at[at], c_r.at[gg, jj], (g, j, cp)))
 
     start(copy(unit, unit, ys.at[0], yr.at[j], (1 - g, j, m)))
+    spread(g, j, 0)
 
     for b in (cp, xcp):
         copy(emb_ref, embf.at[b], es.at[0], er.at[b], (g, j, xp)).wait_recv()
@@ -233,7 +206,7 @@
     cid = lax.broadcasted_iota(jnp.int32, (step, step), 1) // tile
     same = rid == cid
 
-    def encode(r, carry):
+    def encode(r):
         at = pl.ds(pl.multiple_of(r * step, step), step)
         x = [embf[n, at, :][:, :blk].astype(f32) for n in range(N)]
         mean = sum(jnp.sum(v, axis=-1, keepdims=True) for v in x) / (N * blk)
@@ -264,31 +237,52 @@
             wts = (e / jnp.sum(e, axis=-1, keepdims=True)).astype(bf16)
             c = jnp.dot(wts, parts[2][:, hs], preferred_element_type=f32).astype(bf16)
             ctx = ctx + jnp.dot(c, selt_ref[h * 128:(h + 1) * 128, :], preferred_element_type=f32)
-        ctxs[at, :] = ctx.astype(bf16)
-        return carry
-
-    lax.fori_loop(0, rows // step, encode, 0)
-    routed(ctxs[...], csend, ctxr, cs, cr)
-    routed(emb_own, esend, embr, ms, mr)
-
-    start(copy(wout_ref, woutf.at[m], os.at[0], orr.at[m], (g, j, xp)))
-    start(copy(wout_ref, woutf.at[m], os.at[1], orr.at[m], (g, j, cp)))
-    woutf[m] = wout_ref[...]
-    order = [0, 1, 3, 2]
-    spread(g, j, 0)
-    for k in order[1:]:
-        jj = lax.rem(j + k, N)
-        u = wall.at[g, jj, mine, :]
-        copy(u, u, zs.at[k], zr.at[jj], (g, j, xp)).wait_recv()
-        start(copy(u, u, ys.at[k], yr.at[jj], (1 - g, j, m)))
-        spread(g, jj, k)
+        return jnp.dot(ctx.astype(bf16), wout_ref[...], preferred_element_type=f32)
+
+    order = (0, 1, 3, 2)
+    for k in (2, 3, 1):
+        to = lax.rem(m + k, N)
+        asrc[k] = encode(to).astype(bf16)
+        start(copy(asrc.at[k], abuf.at[m], as_s.at[k], as_r.at[m], (g, j, to)))
+        if k != 2:
+            zk = 4 - k
+            jj = lax.rem(j + zk, N)
+            u = wall.at[g, jj, mine, :]
+            copy(u, u, zs.at[zk], zr.at[jj], (g, j, xp)).wait_recv()
+            start(copy(u, u, ys.at[zk], yr.at[jj], (1 - g, j, m)))
+            spread(g, jj, zk)
+    total = encode(m)
+    jj = lax.rem(j + 2, N)
+    u = wall.at[g, jj, mine, :]
+    copy(u, u, zs.at[2], zr.at[jj], (g, j, xp)).wait_recv()
+    start(copy(u, u, ys.at[2], yr.at[jj], (1 - g, j, m)))
+    spread(g, jj, 2)
+
+    for k in (1, 3, 2):
+        frm = lax.rem(m + k, N)
+        copy(asrc.at[k], abuf.at[frm], as_s.at[k], as_r.at[frm], (g, j, frm)).wait_recv()
+        total = total + abuf[frm].astype(f32)
+    at = pl.ds(pl.multiple_of(m * step, step), step)
+    rows_own = jnp.concatenate([embf[n, at, :][:, :blk].astype(f32) for n in range(N)], axis=1)
+    encg[j, :step, :] = (rows_own + total).astype(bf16)
+    encg[j, step:, :] = trow_ref[...]
+    for k in (2, 1, 3):
+        start(copy(encg.at[j], encg.at[j], gs.at[k], gr.at[j], (g, lax.rem(j + k, N), m)))
+
     for k in order:
         jj = lax.rem(j + k, N)
         u = wall.at[1 - g, jj, mine, :]
         copy(u, u, ys.at[k], yr.at[jj], (1 - g, j, m)).wait_recv()
-        spread(1 - g, jj, N + k)
-    copy(wout_ref, woutf.at[xp], os.at[0], orr.at[xp], (g, j, xp)).wait_recv()
-    start(copy(woutf.at[xp], woutf.at[xp], os.at[2], orr.at[xp], (g, j, cp)))
+        spread(1 - g, jj, N + k, k < 2)
+
+    for k in (1, 3, 2):
+        frm = lax.rem(j + k, N)
+        copy(encg.at[j], encg.at[frm], gs.at[k], gr.at[frm], (g, frm, m)).wait_recv()
+    for k in (2, 3, 1):
+        to = lax.rem(m + k, N)
+        start(copy(encg.at[to], fin.at[m], fs.at[k], fr.at[m], (g, j, to)))
+    fin[m] = encg[m]
+
     units = [(gg, k) for gg in range(2) for k in order]
     for gg, k in units:
         ga = g if gg == 0 else 1 - g
@@ -296,18 +290,23 @@
         u = wall.at[ga, jj, xrow, :]
         copy(u, u, xs.at[gg * N + k], xr.at[ga, jj], (g, j, xp)).wait_recv()
         start(copy(u, u, c_s.at[8 + gg * N + k], c_r.at[2 + ga, jj], (g, j, cp)))
-
-    routed_arrived(csend, ctxr, cs, cr)
-    routed_arrived(esend, embr, ms, mr)
-    for b in (cp, xcp):
-        copy(wout_ref, woutf.at[b], os.at[0], orr.at[b], (g, j, xp)).wait_recv()
-    enc = []
-    for n in range(N):
-        acc = jnp.zeros((slots, blk), f32)
-        for k in range(N):
-            acc = acc + jnp.dot(ctxr[k], woutf[k, n], preferred_element_type=f32)
-        enc.append((embr[n][:, :blk].astype(f32) + acc).astype(bf16))
-    used = embr[0][:, blk:blk + 1].astype(f32) > 0.5
+        if gg == 0 and k >= 2:
+            start(copy(u, u, xs.at[N + k], xr.at[g, jj], (1 - g, j, m)))
+
+    place = (lax.broadcasted_iota(jnp.int32, (slots, step), 0) + j * slots).astype(f32)
+    patch = lax.rem(lax.broadcasted_iota(jnp.int32, (1, step), 1), tile).astype(f32)
+    acc = jnp.zeros((slots, N * blk), f32)
+    count = jnp.zeros((slots, 1), f32)
+    for k in (0, 1, 3, 2):
+        frm = lax.rem(m + k, N)
+        if k:
+            copy(encg.at[j], fin.at[frm], fs.at[k], fr.at[frm], (g, j, frm)).wait_recv()
+        goal = fin[frm, step:, :][:1, :step].astype(f32) * tile + patch
+        hot = (place == goal).astype(f32)
+        count = count + jnp.sum(hot, axis=-1, keepdims=True)
+        acc = acc + jnp.dot(hot.astype(bf16), fin[frm, :step, :], preferred_element_type=f32)
+    enc = acc.astype(bf16)
+    used = count > 0.5
 
     for gg, k in units:
         ga = g if gg == 0 else 1 - g
@@ -315,11 +314,7 @@
         for b, row in ((0, crow), (2, xcrow)):
             u = wall.at[ga, jj, row, :]
             copy(u, u, c_s.at[0], c_r.at[b + ga, jj], (g, j, cp)).wait_recv()
-        acc = jnp.zeros((slots, half), f32)
-        for n in range(N):
-            acc = acc + jnp.dot(
-                enc[n], wall[ga, jj, n * blk:(n + 1) * blk, :], preferred_element_type=f32
-            )
+        acc = jnp.dot(enc, wall[ga, jj], preferred_element_type=f32)
         key = (2 * jj + ga) * half < KVD
         for s in range(half // DEC_HD):
             p = acc[:, s * DEC_HD:(s + 1) * DEC_HD]
@@ -331,8 +326,6 @@
 
     for c in pending:
         c.wait_send()
-    routed_sent(csend, ctxr, cs, cr)
-    routed_sent(esend, embr, ms, mr)
 
 
 def per_device_kernel(
@@ -355,9 +348,11 @@
     dest_hot = (destination[:, None] == jnp.arange(N)[None, :]).astype(jnp.int32)
     earlier = jnp.cumsum(dest_hot, axis=0) - dest_hot
     target = destination * cap + jnp.sum(earlier * dest_hot, axis=1)
-    tgt = (target[:, None] * patches + jnp.arange(patches)[None, :]).reshape(1, rows)
+    per = tiles // N
+    trow = jnp.repeat(target.reshape(N, per), patches, axis=1)
+    trow = lax.dynamic_slice_in_dim(trow, lax.axis_index("mp"), 1, 0).astype(bf16)
+    trow = jnp.broadcast_to(jnp.pad(trow, ((0, 0), (0, width - per * patches))), (16, width))
     wqkv = w_qkv.transpose(1, 0, 2)
-    wout = w_out.reshape(blk, N, blk).transpose(1, 0, 2)
     sel = jnp.asarray(selector(), bf16)
     selt = jnp.asarray(selector().T, bf16)
     vm = pl.BlockSpec(memory_space=pltpu.VMEM)
@@ -369,17 +364,15 @@
         out_specs=vm,
         scratch_shapes=[
             pltpu.VMEM((N, rows, lanes), bf16),
-            pltpu.VMEM((rows, blk), bf16),
-            pltpu.VMEM((N, slots, blk), bf16),
-            pltpu.VMEM((N, slots, lanes), bf16),
-            pltpu.VMEM((N, slots, blk), bf16),
-            pltpu.VMEM((N, slots, lanes), bf16),
-            pltpu.VMEM((N, N, blk, blk), bf16),
+            pltpu.VMEM((N, rows // N, width), bf16),
+            pltpu.VMEM((N, rows // N, width), bf16),
+            pltpu.VMEM((N, rows // N + 16, width), bf16),
+            pltpu.VMEM((N, rows // N + 16, width), bf16),
             pltpu.VMEM((N, blk, half), bf16),
             pltpu.VMEM((N, blk, half), bf16),
             pltpu.VMEM((blk, half), f32),
             pltpu.VMEM((2, N, width, half), bf16),
-            sem((3,)), sem((N,)), sem((3,)), sem((N,)),
+            sem((3,)), sem((N,)), sem((N,)), sem((N,)),
             sem((N,)), sem((N,)), sem((N,)), sem((N,)), sem((N,)), sem((N,)),
             sem((2 * N,)), sem((2, N)), sem((4 * N,)), sem((4, N)),
             sem((N,)), sem((N,)), sem((N,)), sem((N,)),
@@ -388,7 +381,7 @@
             collective_id=0, has_side_effects=True, vmem_limit_bytes=56 << 20
         ),
     )(
-        emb, tgt, norm_gain.reshape(N, 1, blk), norm_bias.reshape(N, 1, blk), wqkv, wout,
+        emb, trow, norm_gain.reshape(N, 1, blk), norm_bias.reshape(N, 1, blk), wqkv, w_out,
         w_proj, w_kv, key_gain.reshape(1, -1), sel, selt,
     )
     return out.reshape(cap, patches, columns)

time: 140 us -> 121 us (0.86)
  Pallas kernels: 120 us -> 104 us
    pallas_call x1, Pallas kernels: 120 us -> 104 us  [per_device_kernel(): pl.pallas_call(kernel, out_shape=jax.ShapeDtypeStruct((slots, columns), b...]
    reshape x2 -> x1, local copies, waits for them, and re-layouts: 3.6 us -> 0.09 us  [per_device_kernel(): trow = jnp.repeat(target.reshape(N, per), patches, axis=1)]
    unnamed x6 -> x4, local copies, waits for them, and re-layouts: 5.61 us -> 7.57 us
where the time goes in v2:
time: 121 us; the launch traced here: 120 us
  Pallas kernels  104 us (86%)
  local copies, waits for them, and re-layouts  12.1 us (10%)
  other arithmetic  4.06 us (3%)
    pallas_call x1, Pallas kernels, per_device_kernel(): pl.pallas_call(kernel, out_shape=jax.ShapeDtypeStruct((slots, columns), b...  104 us
    unnamed x4, local copies, waits for them, and re-layouts  7.57 us

profile of v2, /device:TPU:9, one launch (start us, length us, event | category | flops | bytes accessed | tf_op | source)
XLA Modules:
  0.0 120.1 jit_solution(12814654153577045372)
XLA Ops:
  0.0 0.0 copy-start
  0.0 0.7 multiply_add_fusion
  0.7 0.7 multiply_reduce_fusion
  1.4 0.1 mul.15
  1.5 1.4 %reshape.27.gain_ref = f32[4,1,320]{2,1,0:T(1,128)} reshape(f32[1280]{0:T(1024)} %param.19) | data formatting | bytes 10240 | tf_op jit(solution)/shard_map/reshape | solution.py:384
  2.8 1.4 %reshape.28.bias_ref = f32[4,1,320]{2,1,0:T(1,128)} reshape(f32[1280]{0:T(1024)} %param.20) | data formatting | bytes 10240 | tf_op jit(solution)/shard_map/reshape | solution.py:384
  4.2 0.7 fusion
  4.9 0.8 select_reduce_fusion
  5.8 0.1 reduce_sum.12
  5.9 0.1 broadcast_in_dim.6
  6.0 0.1 reshape.26
  6.1 0.0 copy-done
  6.1 0.2 fusion.1
  6.3 0.6 broadcast_in_dim.16.trow_ref
  6.9 1.1 add_convert_fusion
  8.0 0.8 pad.8.emb_ref
  8.8 5.3 %copy.15 = bf16[1280,3,320]{2,0,1:T(8,128)(2,1)} copy(bf16[1280,3,320]{0,2,1:T(8,128)(2,1)} %param.21) | data formatting | bytes 4915200 | tf_op args[7]
  14.0 103.8 %shard_map.136 = bf16[256,2048]{1,0:T(8,128)(2,1)} custom-call(bf16[512,384]{1,0:T(8,128)(2,1)} %pad.8.emb_ref, bf16[16,1280]{1,0:T(8,128)(2,1)} %broadcast_in_dim.16.trow_ref, f32[4,1,320]{2,1,0:T(1,128)} %reshape.27.gain_ref, f32[4,1,320]{2,1,0:T(1,128)} %reshape.28.bias_ref, bf16[3,1280,320]{2,1,0:T(8,128)(2,1)} %bitcast.6, bf16[320,1280]{1,0:T(8,128)(2,1)} %wout_ref.1, ...), custom_call_target="tpu_custom_call" | custom-call | tf_op jit(solution)/shard_map/pallas_call | solution.py:360
  117.8 2.3 %copy.17 = bf16[8,32,2048]{2,1,0:T(8,128)(2,1)} copy(bf16[8,32,2048]{2,1,0:T(8,128)(2,1)} %bitcast.7) | data formatting | bytes 2097152
  (4 shorter events, 0.1 us)
Async XLA Ops:
  0.0 6.1 %copy-start = (bf16[16,320]{1,0:T(8,128)(2,1)S(1)}, bf16[16,320]{1,0:T(8,128)(2,1)}, u32[]{:S(2)}) copy-start(bf16[16,320]{1,0:T(8,128)(2,1)} %param.18) | copy-start | bytes 30724

commit v3 on v2

--- a/solution.py
+++ b/solution.py
@@ -213,7 +213,7 @@
         x = [v - mean for v in x]
         var = sum(jnp.sum(v * v, axis=-1, keepdims=True) for v in x) / (N * blk)
         inv = lax.rsqrt(var + 1e-05)
-        x = [(x[n] * inv * gain_ref[n] + bias_ref[n]).astype(bf16) for n in range(N)]
+        x = [(x[n] * inv * gain_ref[:, n * blk:(n + 1) * blk] + bias_ref[:, n * blk:(n + 1) * blk]).astype(bf16) for n in range(N)]
         parts = []
         for k in range(3):
             acc = jnp.zeros((step, blk), f32)
@@ -273,7 +273,21 @@
         jj = lax.rem(j + k, N)
         u = wall.at[1 - g, jj, mine, :]
         copy(u, u, ys.at[k], yr.at[jj], (1 - g, j, m)).wait_recv()
-        spread(1 - g, jj, N + k, k < 2)
+        spread(1 - g, jj, N + k, False)
+
+    units = [(gg, k) for gg in range(2) for k in order]
+
+    def pass_on(gg):
+        for k in order:
+            ga = g if gg == 0 else 1 - g
+            jj = lax.rem(j + k, N)
+            u = wall.at[ga, jj, xrow, :]
+            copy(u, u, xs.at[gg * N + k], xr.at[ga, jj], (g, j, xp)).wait_recv()
+            if gg == 0:
+                start(copy(u, u, xs.at[N + k], xr.at[g, jj], (1 - g, j, m)))
+            start(copy(u, u, c_s.at[8 + gg * N + k], c_r.at[2 + ga, jj], (g, j, cp)))
+
+    pass_on(0)
 
     for k in (1, 3, 2):
         frm = lax.rem(j + k, N)
@@ -283,15 +297,7 @@
         start(copy(encg.at[to], fin.at[m], fs.at[k], fr.at[m], (g, j, to)))
     fin[m] = encg[m]
 
-    units = [(gg, k) for gg in range(2) for k in order]
-    for gg, k in units:
-        ga = g if gg == 0 else 1 - g
-        jj = lax.rem(j + k, N)
-        u = wall.at[ga, jj, xrow, :]
-        copy(u, u, xs.at[gg * N + k], xr.at[ga, jj], (g, j, xp)).wait_recv()
-        start(copy(u, u, c_s.at[8 + gg * N + k], c_r.at[2 + ga, jj], (g, j, cp)))
-        if gg == 0 and k >= 2:
-            start(copy(u, u, xs.at[N + k], xr.at[g, jj], (1 - g, j, m)))
+    pass_on(1)
 
     place = (lax.broadcasted_iota(jnp.int32, (slots, step), 0) + j * slots).astype(f32)
     patch = lax.rem(lax.broadcasted_iota(jnp.int32, (1, step), 1), tile).astype(f32)
@@ -338,12 +344,10 @@
     rows, slots = tiles * patches, cap * patches
     width, columns = w_proj.shape[0], w_kv.shape[1] * N
     half = w_kv.shape[1] // 2
-    lanes = -(-(blk + 1) // 128) * 128
     lookup = (tile_count - 1) * MAXT + tile_order
     lookup_hot = (lookup[:, None] == jnp.arange(MAXT * MAXT)[None, :]).astype(bf16)
     table_rows = jnp.dot(lookup_hot, tile_embed, preferred_element_type=f32)
     emb = (tile_rows.astype(f32) + table_rows[:, None, :]).astype(bf16).reshape(rows, blk)
-    emb = jnp.pad(emb, ((0, 0), (0, lanes - blk)), constant_values=1)
     destination = route[:, 0]
     dest_hot = (destination[:, None] == jnp.arange(N)[None, :]).astype(jnp.int32)
     earlier = jnp.cumsum(dest_hot, axis=0) - dest_hot
@@ -363,7 +367,7 @@
         in_specs=[vm] * 11,
         out_specs=vm,
         scratch_shapes=[
-            pltpu.VMEM((N, rows, lanes), bf16),
+            pltpu.VMEM((N, rows, blk), bf16),
             pltpu.VMEM((N, rows // N, width), bf16),
             pltpu.VMEM((N, rows // N, width), bf16),
             pltpu.VMEM((N, rows // N + 16, width), bf16),
@@ -381,7 +385,7 @@
             collective_id=0, has_side_effects=True, vmem_limit_bytes=56 << 20
         ),
     )(
-        emb, trow, norm_gain.reshape(N, 1, blk), norm_bias.reshape(N, 1, blk), wqkv, w_out,
+        emb, trow, norm_gain.reshape(1, width), norm_bias.reshape(1, width), wqkv, w_out,
         w_proj, w_kv, key_gain.reshape(1, -1), sel, selt,
     )
     return out.reshape(cap, patches, columns)

time: 121 us -> 120 us (level)
  no operation moved by 1% of the time
where the time goes in v3:
time: 120 us
  Pallas kernels  104 us (87%)
  local copies, waits for them, and re-layouts  11.1 us (9%)
  other arithmetic  4.8 us (4%)
    pallas_call x1, Pallas kernels, per_device_kernel(): pl.pallas_call(kernel, out_shape=jax.ShapeDtypeStruct((slots, columns), b...  104 us
    unnamed x4, local copies, waits for them, and re-layouts  7.57 us

profile of v3, /device:TPU:9, one launch (start us, length us, event | category | flops | bytes accessed | tf_op | source)
XLA Modules:
  0.0 120.0 jit_solution(1879048589357200265)
XLA Ops:
  0.0 0.0 copy-start
  0.0 0.7 multiply_add_fusion
  0.7 0.7 multiply_reduce_fusion
  1.4 0.1 mul.15
  1.5 1.3 %reshape.27.gain_ref = f32[1,1280]{1,0:T(1,128)} reshape(f32[1280]{0:T(1024)} %param.19) | data formatting | bytes 10240 | tf_op jit(solution)/shard_map/reshape | solution.py:388
  2.7 1.3 %reshape.28.bias_ref = f32[1,1280]{1,0:T(1,128)} reshape(f32[1280]{0:T(1024)} %param.20) | data formatting | bytes 10240 | tf_op jit(solution)/shard_map/reshape | solution.py:388
  4.0 0.7 fusion
  4.8 0.8 select_reduce_fusion
  5.6 0.1 reduce_sum.12
  5.7 0.1 broadcast_in_dim.6
  5.8 0.1 reshape.26
  5.9 0.0 copy-done
  5.9 0.2 fusion.1
  6.1 0.6 broadcast_in_dim.16.trow_ref
  6.8 1.8 %add_convert_fusion = bf16[16,32,320]{2,1,0:T(8,128)(2,1)} fusion(bf16[16,32,320]{2,1,0:T(8,128)(2,1)} %param.14, f32[16,320]{1,0:T(8,128)S(1)} %fusion.1), kind=kLoop, calls=%fused_computation | loop fusion | flops 491520 | bytes 675840 | tf_op jit(solution)/shard_map/convert_element_type | solution.py:350
  8.6 5.3 %copy.15 = bf16[1280,3,320]{2,0,1:T(8,128)(2,1)} copy(bf16[1280,3,320]{0,2,1:T(8,128)(2,1)} %param.21) | data formatting | bytes 4915200 | tf_op args[7]
  13.8 103.8 %shard_map.136 = bf16[256,2048]{1,0:T(8,128)(2,1)} custom-call(bf16[512,320]{1,0:T(8,128)(2,1)} %bitcast.8, bf16[16,1280]{1,0:T(8,128)(2,1)} %broadcast_in_dim.16.trow_ref, f32[1,1280]{1,0:T(1,128)} %reshape.27.gain_ref, f32[1,1280]{1,0:T(1,128)} %reshape.28.bias_ref, bf16[3,1280,320]{2,1,0:T(8,128)(2,1)} %bitcast.6, bf16[320,1280]{1,0:T(8,128)(2,1)} %wout_ref.1, ...), custom_call_target="tpu_custom_call" | custom-call | tf_op jit(solution)/shard_map/pallas_call | solution.py:364
  117.7 2.3 %copy.17 = bf16[8,32,2048]{2,1,0:T(8,128)(2,1)} copy(bf16[8,32,2048]{2,1,0:T(8,128)(2,1)} %bitcast.7) | data formatting | bytes 2097152
  (4 shorter events, 0.1 us)
Async XLA Ops:
  0.0 5.9 %copy-start = (bf16[16,320]{1,0:T(8,128)(2,1)S(1)}, bf16[16,320]{1,0:T(8,128)(2,1)}, u32[]{:S(2)}) copy-start(bf16[16,320]{1,0:T(8,128)(2,1)} %param.18) | copy-start | bytes 30724

commit v4 on v3

--- a/solution.py
+++ b/solution.py
@@ -117,7 +117,7 @@
 
 
 def kernel(
-    emb_ref, trow_ref, gain_ref, bias_ref, wqkv_ref, wout_ref, wproj_ref, wkv_ref, kgain_ref,
+    emb_ref, trow_ref, norm_ref, wqkv_ref, wout_ref, wproj_ref, wkv_ref, kgain_ref,
     sel_ref, selt_ref, out_ref,
     embf, asrc, abuf, encg, fin, rssrc, rsbuf, own, wall,
     es, er, as_s, as_r, rs_s, rs_r, zs, zr, ys, yr, xs, xr, c_s, c_r, gs, gr, fs, fr,
@@ -213,7 +213,7 @@
         x = [v - mean for v in x]
         var = sum(jnp.sum(v * v, axis=-1, keepdims=True) for v in x) / (N * blk)
         inv = lax.rsqrt(var + 1e-05)
-        x = [(x[n] * inv * gain_ref[:, n * blk:(n + 1) * blk] + bias_ref[:, n * blk:(n + 1) * blk]).astype(bf16) for n in range(N)]
+        x = [(x[n] * inv * norm_ref[0:1, n * blk:(n + 1) * blk] + norm_ref[1:2, n * blk:(n + 1) * blk]).astype(bf16) for n in range(N)]
         parts = []
         for k in range(3):
             acc = jnp.zeros((step, blk), f32)
@@ -364,7 +364,7 @@
     out = pl.pallas_call(
         kernel,
         out_shape=jax.ShapeDtypeStruct((slots, columns), bf16),
-        in_specs=[vm] * 11,
+        in_specs=[vm] * 10,
         out_specs=vm,
         scratch_shapes=[
             pltpu.VMEM((N, rows, blk), bf16),
@@ -385,7 +385,7 @@
             collective_id=0, has_side_effects=True, vmem_limit_bytes=56 << 20
         ),
     )(
-        emb, trow, norm_gain.reshape(1, width), norm_bias.reshape(1, width), wqkv, w_out,
+        emb, trow, jnp.stack([norm_gain, norm_bias]), wqkv, w_out,
         w_proj, w_kv, key_gain.reshape(1, -1), sel, selt,
     )
     return out.reshape(cap, patches, columns)

time: 120 us -> 120 us (level)
    reshape x2 -> x0, local copies, waits for them, and re-layouts: 2.59 us -> none  [the longest x1 1.29 us: per_device_kernel(): norm_gain.reshape(1, width)]
    another operation x0 -> x2, local copies, waits for them, and re-layouts: none -> 1.4 us  [per_device_kernel(): jnp.stack([norm_gain, norm_bias])]
where the time goes in v4:
time: 120 us; the launch traced here: 119 us
  Pallas kernels  104 us (87%)
  local copies, waits for them, and re-layouts  9.95 us (8%)
  other arithmetic  5.41 us (5%)
    pallas_call x1, Pallas kernels, per_device_kernel(): pl.pallas_call(kernel, out_shape=jax.ShapeDtypeStruct((slots, columns), b...  104 us
    unnamed x4, local copies, waits for them, and re-layouts  7.57 us

profile of v4, /device:TPU:9, one launch (start us, length us, event | category | flops | bytes accessed | tf_op | source)
XLA Modules:
  0.0 119.4 jit_solution(9841467589839973788)
XLA Ops:
  0.0 0.0 copy-start
  0.0 0.7 multiply_add_fusion
  0.7 0.7 multiply_reduce_fusion
  1.4 0.1 mul.15
  1.5 0.7 stack.9
  2.2 0.7 stack.10
  2.9 0.6 pad_maximum_fusion.norm_ref
  3.5 0.7 fusion
  4.2 0.8 select_reduce_fusion
  5.1 0.1 reduce_sum.12
  5.2 0.1 broadcast_in_dim.6
  5.2 0.1 reshape.20
  5.4 0.0 copy-done
  5.4 0.2 fusion.1
  5.6 0.6 broadcast_in_dim.16.trow_ref
  6.2 1.8 %add_convert_fusion = bf16[16,32,320]{2,1,0:T(8,128)(2,1)} fusion(bf16[16,32,320]{2,1,0:T(8,128)(2,1)} %param.14, f32[16,320]{1,0:T(8,128)S(1)} %fusion.1), kind=kLoop, calls=%fused_computation | loop fusion | flops 491520 | bytes 675840 | tf_op jit(solution)/shard_map/convert_element_type | solution.py:350
  8.0 5.3 %copy.15 = bf16[1280,3,320]{2,0,1:T(8,128)(2,1)} copy(bf16[1280,3,320]{0,2,1:T(8,128)(2,1)} %param.21) | data formatting | bytes 4915200 | tf_op args[7]
  13.3 103.8 %shard_map.136 = bf16[256,2048]{1,0:T(8,128)(2,1)} custom-call(bf16[512,320]{1,0:T(8,128)(2,1)} %bitcast.8, bf16[16,1280]{1,0:T(8,128)(2,1)} %broadcast_in_dim.16.trow_ref, f32[2,1280]{1,0:T(2,128)} %pad_maximum_fusion.norm_ref, bf16[3,1280,320]{2,1,0:T(8,128)(2,1)} %bitcast.6, bf16[320,1280]{1,0:T(8,128)(2,1)} %wout_ref.1, bf16[1280,2048]{1,0:T(8,128)(2,1)} %wproj_ref.1, ...), custom_call_target="tpu_custom_call" | custom-call | tf_op jit(solution)/shard_map/pallas_call | solution.py:364
  117.1 2.3 %copy.17 = bf16[8,32,2048]{2,1,0:T(8,128)(2,1)} copy(bf16[8,32,2048]{2,1,0:T(8,128)(2,1)} %bitcast.7) | data formatting | bytes 2097152
  (4 shorter events, 0.1 us)
Async XLA Ops:
  0.0 5.4 %copy-start = (bf16[16,320]{1,0:T(8,128)(2,1)S(1)}, bf16[16,320]{1,0:T(8,128)(2,1)}, u32[]{:S(2)}) copy-start(bf16[16,320]{1,0:T(8,128)(2,1)} %param.18) | copy-start | bytes 30724
